TPU v7x, 32 devices: a whole 2x2x4 slice. The times are simulated.
32 devices in a mesh: seq: 8 (over y, x, core), head: 4 (over z).
Axes of the slice: x: 2, y: 2, z: 4, core: 2. Of those that a mesh axis runs over, the one named last changes fastest.
Arguments:
- query_rows: bfloat16 [2048, 8, 128], P('seq', 'head'), may hold values from -20 to 20
- key_rows: bfloat16 [2048, 8, 128], P('seq', 'head'), may hold values from -20 to 20
- value_rows: bfloat16 [2048, 8, 128], P('seq', 'head'), may hold values from -6 to 6
- cotangent: bfloat16 [2048, 8, 128], P('seq', 'head'), may hold values from -6 to 6
- norm_gain: float32 [8, 128], P('head'), may hold values from 0.5 to 2
- offsets: int32 [8], P('head'), may hold values from 0 to 31, as said below
Outputs:
- query_grad: bfloat16 [2048, 8, 128], P('seq', 'head')
- key_grad: bfloat16 [2048, 8, 128], P('seq', 'head')
- value_grad: bfloat16 [2048, 8, 128], P('seq', 'head')
Inputs may be any that keep to these rules, and one draw needn't show every extreme that they name: The heads' offsets are distinct.
All inputs are finite; a program needn't handle non-finite values.
Results may differ from a plain program's by a relative error of at most 0.018.
Values may be sent and summed in bfloat16 or wider, within the bound.
A program may use at most 128 MiB of HBM per device.

v0:
```python
import functools

import jax
import jax.numpy as jnp
from jax import lax
from jax.experimental import pallas as pl
from jax.experimental.pallas import tpu as pltpu
from jax.sharding import PartitionSpec as P

RATE2 = 4
RATE3 = 16
RATE4 = 32


neg_fill = -1e30
epsilon = 1e-05
block_width = 512


def passed_along(value, axis, steps):
    count = lax.axis_size(axis)
    leading, last = (max(0, -steps), min(count, count - steps))
    return lax.ppermute(value, axis, [(source, source + steps) for source in range(leading, last)])


def pick_rows(source, wanted, stride):
    row_count = source.shape[0] // stride
    shaped = source.reshape((row_count, stride) + source.shape[1:])
    trailing = (1,) * (source.ndim - 2)
    target = wanted.reshape((1, 1, -1) + trailing)
    column = jnp.arange(stride, dtype=jnp.int32).reshape((1, stride, 1) + trailing)
    zeroed = jnp.where(column == target, shaped, jnp.zeros((), source.dtype))
    return jnp.sum(zeroed, axis=1, dtype=source.dtype)


def put_rows(compact, wanted, stride, filler):
    trailing = (1,) * (compact.ndim - 2)
    target = wanted.reshape((1, 1, -1) + trailing)
    column = jnp.arange(stride, dtype=jnp.int32).reshape((1, stride, 1) + trailing)
    spread = jnp.where(column == target, compact[:, None], jnp.asarray(filler, compact.dtype))
    return spread.reshape((compact.shape[0] * stride,) + compact.shape[1:])


def row_places(device, slot_count, direction, row_count, stride, wanted, tok_dev):
    owners = device + direction * jnp.arange(slot_count, dtype=jnp.int32)
    within_dev = wanted[None, :] + stride * jnp.arange(row_count, dtype=jnp.int32)[:, None]
    places = owners[:, None, None] * tok_dev + within_dev[None]
    return places.reshape(slot_count * row_count, wanted.shape[0])


def masked_scores(query_blk, key_blk, query_pos, key_pos, seg_len, score_scale):
    raw = (
        jnp.einsum("qhd,khd->hqk", query_blk, key_blk, preferred_element_type=jnp.float32)
        * score_scale
    )
    query_at = query_pos.T[:, :, None]
    key_at = key_pos.T[:, None, :]
    linked = (query_at // seg_len == key_at // seg_len) & (key_at <= query_at)
    return jnp.where(linked, raw, neg_fill)


def flatten_slots(member):
    return member.reshape((member.shape[0] * member.shape[1],) + member.shape[2:])


def extend(buffers, target, sign, puller):
    while buffers[0].shape[0] < target:
        covered = buffers[0].shape[0]
        arrived = puller(buffers, sign * covered)
        buffers = tuple(
            (jnp.concatenate([held, current], axis=0) for held, current in zip(buffers, arrived))
        )
    return buffers


def pull_keys(buffers, offset):
    return passed_along((buffers[0], buffers[1]), "seq", offset)


def pull_queries(buffers, offset):
    moved = passed_along((buffers[0], buffers[1]), "seq", offset)
    stats = passed_along((buffers[2], buffers[3]), "seq", offset)
    return (moved[0], moved[1], stats[0], stats[1])


def feature_sums(first, second):
    return lax.psum((first, second), "head")


def shards(query_rows, key_rows, value_rows, cotangent, norm_gain, offsets):
    tok_dev, heads_dev, head_size = query_rows.shape
    seq_count = lax.axis_size("seq")
    device = lax.axis_index("seq")
    group_rows = tok_dev * seq_count // RATE4
    score_scale = head_size ** (-0.5)
    features = heads_dev * head_size * lax.axis_size("head")
    levels = []
    for stride in (1, RATE2, RATE3, RATE4):
        seg_len = stride * group_rows
        levels.append((stride, seg_len, max(1, seg_len // tok_dev), offsets % stride))
    key_sets = []
    for stride, seg_len, span_devices, wanted in levels:
        own_rows = (
            pick_rows(key_rows, wanted, stride)[None],
            pick_rows(value_rows, wanted, stride)[None],
        )
        key_sets.append(extend(own_rows, span_devices, 1, pull_keys))
    prepared = []
    for (stride, seg_len, span_devices, wanted), key_set in zip(levels, key_sets):
        row_count = tok_dev // stride
        key_flat = flatten_slots(key_set[0])
        value_flat = flatten_slots(key_set[1])
        key_places = row_places(device, key_set[0].shape[0], -1, row_count, stride, wanted, tok_dev)
        query_sel = pick_rows(query_rows, wanted, stride)
        query_places = row_places(device, 1, -1, row_count, stride, wanted, tok_dev)
        prepared.append(
            (
                stride,
                seg_len,
                span_devices,
                wanted,
                row_count,
                key_flat,
                value_flat,
                key_places,
                query_sel,
                query_places,
            )
        )
    lse_total = jnp.full((tok_dev, heads_dev), neg_fill, jnp.float32)
    for (
        stride,
        seg_len,
        span_devices,
        wanted,
        row_count,
        key_flat,
        value_flat,
        key_places,
        query_sel,
        query_places,
    ) in prepared:
        level_lse = jnp.full((row_count, heads_dev), neg_fill, jnp.float32)
        for first_row in range(0, key_flat.shape[0], block_width):
            scores = masked_scores(
                query_sel,
                key_flat[first_row : first_row + block_width],
                query_places,
                key_places[first_row : first_row + block_width],
                seg_len,
                score_scale,
            )
            row_peak = jnp.max(scores, axis=2)
            block_lse = row_peak + jnp.log(jnp.sum(jnp.exp(scores - row_peak[:, :, None]), axis=2))
            level_lse = jnp.logaddexp(level_lse, block_lse.T)
        lse_total = jnp.logaddexp(lse_total, put_rows(level_lse, wanted, stride, neg_fill))
    attended = jnp.zeros((tok_dev, heads_dev, head_size), jnp.float32)
    for (
        stride,
        seg_len,
        span_devices,
        wanted,
        row_count,
        key_flat,
        value_flat,
        key_places,
        query_sel,
        query_places,
    ) in prepared:
        lse_sel = pick_rows(lse_total, wanted, stride)
        out_sel = jnp.zeros((row_count, heads_dev, head_size), jnp.float32)
        for first_row in range(0, key_flat.shape[0], block_width):
            scores = masked_scores(
                query_sel,
                key_flat[first_row : first_row + block_width],
                query_places,
                key_places[first_row : first_row + block_width],
                seg_len,
                score_scale,
            )
            weights = jnp.exp(scores - lse_sel.T[:, :, None]).astype(jnp.bfloat16)
            out_sel = out_sel + jnp.einsum(
                "hqk,khd->qhd",
                weights,
                value_flat[first_row : first_row + block_width],
                preferred_element_type=jnp.float32,
            )
        attended = attended + put_rows(out_sel, wanted, stride, 0.0)
    totals = feature_sums(jnp.sum(attended, axis=(1, 2)), jnp.sum(attended * attended, axis=(1, 2)))
    centre = totals[0] / features
    variance = totals[1] / features - centre * centre
    inverse = lax.rsqrt(variance + epsilon)
    normed = (attended - centre[:, None, None]) * inverse[:, None, None]
    grad_in = cotangent.astype(jnp.float32) * norm_gain[None]
    moments = feature_sums(jnp.sum(grad_in, axis=(1, 2)), jnp.sum(grad_in * normed, axis=(1, 2)))
    first_mean = moments[0] / features
    second_mean = moments[1] / features
    d_attended = (
        inverse[:, None, None]
        * (grad_in - first_mean[:, None, None] - normed * second_mean[:, None, None])
    ).astype(jnp.bfloat16)
    row_delta = jnp.sum(d_attended.astype(jnp.float32) * attended, axis=2)
    query_grad = jnp.zeros((tok_dev, heads_dev, head_size), jnp.float32)
    for (
        stride,
        seg_len,
        span_devices,
        wanted,
        row_count,
        key_flat,
        value_flat,
        key_places,
        query_sel,
        query_places,
    ) in prepared:
        lse_sel = pick_rows(lse_total, wanted, stride)
        dout_sel = pick_rows(d_attended, wanted, stride)
        delta_sel = pick_rows(row_delta, wanted, stride)
        grad_sel = jnp.zeros((row_count, heads_dev, head_size), jnp.float32)
        for first_row in range(0, key_flat.shape[0], block_width):
            key_block = key_flat[first_row : first_row + block_width]
            scores = masked_scores(
                query_sel,
                key_block,
                query_places,
                key_places[first_row : first_row + block_width],
                seg_len,
                score_scale,
            )
            weights = jnp.exp(scores - lse_sel.T[:, :, None])
            weight_grad = jnp.einsum(
                "qhd,khd->hqk",
                dout_sel,
                value_flat[first_row : first_row + block_width],
                preferred_element_type=jnp.float32,
            )
            score_grad = (weights * (weight_grad - delta_sel.T[:, :, None])).astype(jnp.bfloat16)
            grad_sel = grad_sel + jnp.einsum(
                "hqk,khd->qhd", score_grad, key_block, preferred_element_type=jnp.float32
            )
        query_grad = query_grad + put_rows(grad_sel * score_scale, wanted, stride, 0.0)
    query_sets = []
    for stride, seg_len, span_devices, wanted in levels:
        own_rows = (
            pick_rows(query_rows, wanted, stride)[None],
            pick_rows(d_attended, wanted, stride)[None],
            pick_rows(lse_total, wanted, stride)[None],
            pick_rows(row_delta, wanted, stride)[None],
        )
        query_sets.append(extend(own_rows, span_devices, -1, pull_queries))
    key_grad = jnp.zeros((tok_dev, heads_dev, head_size), jnp.float32)
    value_grad = jnp.zeros((tok_dev, heads_dev, head_size), jnp.float32)
    for (
        stride,
        seg_len,
        span_devices,
        wanted,
        row_count,
        key_flat,
        value_flat,
        key_places,
        query_sel,
        query_places,
    ), query_set in zip(prepared, query_sets):
        query_flat = flatten_slots(query_set[0])
        dout_flat = flatten_slots(query_set[1])
        lse_flat = flatten_slots(query_set[2])
        delta_flat = flatten_slots(query_set[3])
        query_far = row_places(device, query_set[0].shape[0], 1, row_count, stride, wanted, tok_dev)
        key_sel = pick_rows(key_rows, wanted, stride)
        value_sel = pick_rows(value_rows, wanted, stride)
        key_grad_sel = jnp.zeros((row_count, heads_dev, head_size), jnp.float32)
        value_grad_sel = jnp.zeros((row_count, heads_dev, head_size), jnp.float32)
        for first_row in range(0, query_flat.shape[0], block_width):
            query_block = query_flat[first_row : first_row + block_width]
            dout_block = dout_flat[first_row : first_row + block_width]
            lse_block = lse_flat[first_row : first_row + block_width]
            delta_block = delta_flat[first_row : first_row + block_width]
            scores = masked_scores(
                query_block,
                key_sel,
                query_far[first_row : first_row + block_width],
                query_places,
                seg_len,
                score_scale,
            )
            weights = jnp.exp(scores - lse_block.T[:, :, None])
            value_grad_sel = value_grad_sel + jnp.einsum(
                "hqk,qhd->khd",
                weights.astype(jnp.bfloat16),
                dout_block,
                preferred_element_type=jnp.float32,
            )
            weight_grad = jnp.einsum(
                "qhd,khd->hqk", dout_block, value_sel, preferred_element_type=jnp.float32
            )
            score_grad = (weights * (weight_grad - delta_block.T[:, :, None])).astype(jnp.bfloat16)
            key_grad_sel = key_grad_sel + jnp.einsum(
                "hqk,qhd->khd", score_grad, query_block, preferred_element_type=jnp.float32
            )
        key_grad = key_grad + put_rows(key_grad_sel * score_scale, wanted, stride, 0.0)
        value_grad = value_grad + put_rows(value_grad_sel, wanted, stride, 0.0)
    return (
        query_grad.astype(jnp.bfloat16),
        key_grad.astype(jnp.bfloat16),
        value_grad.astype(jnp.bfloat16),
    )

MESH = pl.DeviceIdType.MESH
LOG2E = 1.4426950408889634
HIDDEN = -1e30
ROWS = 16
VMEM_BYTES = 54752 * 1024


def dot_nn(a, b):
    return lax.dot_general(a, b, (((1,), (0,)), ((), ())), preferred_element_type=jnp.float32)


def dot_nt(a, b):
    return lax.dot_general(a, b, (((1,), (1,)), ((), ())), preferred_element_type=jnp.float32)


def dot_tn(a, b):
    return lax.dot_general(a, b, (((0,), (0,)), ((), ())), preferred_element_type=jnp.float32)


def iota(shape, axis):
    return lax.broadcasted_iota(jnp.int32, shape, axis)


def bias_of(count):
    return jnp.where(count > 0.5, jnp.log2(jnp.maximum(count, 1.0)), HIDDEN)


def fused(
    seqs,
    heads,
    seg1,
    features,
    off_hbm,
    q_hbm,
    k_hbm,
    v_hbm,
    c_hbm,
    gain_hbm,
    dq_ref,
    dk_ref,
    dv_ref,
    off_ref,
    gain_ref,
    xin,
    wide,
    mats,
    grads,
    weights,
    far_weights,
    bias,
    far_bias,
    late_score,
    picker,
    placer,
    kvsel,
    qsel,
    dosel,
    kvbuf,
    qbuf,
    dobuf,
    hsend,
    hbuf,
    rows_ref,
    outwide,
    in_sem,
    kv_send,
    kv_recv,
    q_send,
    q_recv,
    do_send,
    do_recv,
    h_send,
    h_recv,
):
    me = lax.axis_index("seq")
    mine = lax.axis_index("head")
    both, tok = mats.shape[1], mats.shape[2]
    size = mats.shape[3]
    far = seqs * ROWS
    half = ROWS // 2
    quad = RATE3 * seg1 // tok
    scale = size ** (-0.5)
    scale2 = scale * LOG2E

    loads = []
    for at, (source, target) in enumerate(
        (
            (off_hbm, off_ref),
            (k_hbm, xin.at[0]),
            (v_hbm, xin.at[1]),
            (q_hbm, xin.at[2]),
            (c_hbm, xin.at[3]),
            (gain_hbm, gain_ref),
        )
    ):
        copy = pltpu.make_async_copy(source, target, in_sem.at[at])
        copy.start()
        loads.append(copy)
    kvbuf[...] = jnp.zeros_like(kvbuf)
    qbuf[...] = jnp.zeros_like(qbuf)
    dobuf[...] = jnp.zeros_like(dobuf)
    hbuf[...] = jnp.zeros_like(hbuf)

    barrier = pltpu.get_barrier_semaphore()
    for step in range(1, seqs):
        pl.semaphore_signal(
            barrier, inc=1, device_id=(lax.rem(me + step, seqs), mine), device_id_type=MESH
        )
    for step in range(1, heads):
        pl.semaphore_signal(
            barrier, inc=1, device_id=(me, lax.rem(mine + step, heads)), device_id_type=MESH
        )
    rows_ref[...] = jnp.zeros_like(rows_ref)

    def remote(source, target, send, recv, step, owner):
        return pltpu.make_async_remote_copy(
            src_ref=source,
            dst_ref=target,
            send_sem=send.at[step - 1],
            recv_sem=recv.at[step - 1],
            device_id=owner,
            device_id_type=MESH,
        )

    def peer(step):
        owner = me
        for bit in range(step.bit_length()):
            if (step >> bit) & 1:
                owner = owner + 2**bit * (1 - 2 * ((me // 2**bit) % 2))
        return (owner, mine)

    kv_copies, q_copies, do_copies = {}, {}, {}
    for step in range(1, seqs):
        count = 2 * ROWS if step < quad else ROWS
        top = pl.ds(0, count)
        kv_copies[step] = remote(
            kvsel.at[:, top], kvbuf.at[:, me, top], kv_send, kv_recv, step, peer(step)
        )
        q_copies[step] = remote(qsel.at[top], qbuf.at[me, top], q_send, q_recv, step, peer(step))
        top = pl.ds(0, count + ROWS)
        do_copies[step] = remote(
            dosel.at[top], dobuf.at[me, top], do_send, do_recv, step, peer(step)
        )
    h_copies = [
        remote(hsend, hbuf.at[mine], h_send, h_recv, step, (me, lax.rem(mine + step, heads)))
        for step in range(1, heads)
    ]

    def each(side, copies, action):
        width = seqs // 2
        while width:
            @pl.when((me // width) % 2 == side)
            def _(width=width):
                for step in range(width, 2 * width):
                    getattr(copies[step], action)()

            width //= 2

    def per_head(mixed, h):
        groups = mixed.astype(jnp.float32).reshape(seqs, 2, both, half, size)
        return groups[:, :, h].reshape(far, size).astype(jnp.bfloat16)

    def select(at, g):
        rows = []
        for h in range(both):
            start = both * ((wanted[h] & (RATE4 - 1)) ^ (RATE3 * g)) + h
            rows.append(wide[at, pl.ds(start, half, stride=both * RATE4), :])
        return jnp.concatenate(rows, axis=0).astype(jnp.bfloat16)

    loads[0].wait()
    wanted = [off_ref[h] for h in range(both)]

    lane = iota((tok, 128), 1)
    token = iota((tok, 128), 0)
    causal = iota((tok, tok), 0) <= iota((tok, tok), 1)
    for h in range(both):
        off = wanted[h]
        marks = (token // seg1) == lane
        marks = marks | ((lane == 64) & ((token & (RATE2 - 1)) == (off & (RATE2 - 1))))
        marks = marks | ((lane == 65) & ((token & (RATE3 - 1)) == (off & (RATE3 - 1))))
        marks = marks | ((lane == 66) & ((token & (RATE4 - 1)) == (off & (RATE4 - 1))))
        marked = jnp.where(marks, 1.0, 0.0).astype(jnp.bfloat16)
        count = dot_nt(marked, marked)
        bias[h] = bias_of(jnp.where(causal, count, 0.0))

    for at in range(2):
        loads[1 + at].wait()
        wide[at] = xin[at].astype(jnp.float32)
        for g in range(2):
            kvsel[at, pl.ds(g * ROWS, ROWS), :] = select(at, g)
    pl.semaphore_wait(barrier, seqs + heads - 2)
    each(0, kv_copies, "start")

    loads[3].wait()
    wide[2] = xin[2].astype(jnp.float32)
    for g in range(2):
        qsel[pl.ds(g * ROWS, ROWS), :] = select(2, g)
    each(1, q_copies, "start")

    for at in range(3):
        for h in range(both):
            mats[at, h] = wide[at, pl.ds(h, tok, stride=both), :].astype(jnp.bfloat16)

    first_stats = []
    for h in range(both):
        score = dot_nt(mats[0, h], mats[2, h]) * scale2 + bias[h]
        peak = jnp.max(score, axis=0, keepdims=True)
        held = jnp.exp2(score - peak)
        weights[h] = held
        total = jnp.sum(held, axis=0, keepdims=True)
        out = dot_tn(mats[1, h], held.astype(jnp.bfloat16))
        first_stats.append((peak, total, out))

    loads[4].wait()
    loads[5].wait()
    wide[3] = xin[3].astype(jnp.float32)
    for h in range(both):
        grad = wide[3, pl.ds(h, tok, stride=both), :] * gain_ref[h : h + 1, :]
        grads[h] = grad.T

    for h in range(both):
        off = wanted[h]
        slot = iota((far, tok), 0) // ROWS
        query = iota((far, tok), 1)
        sel3 = (query & (RATE3 - 1)) == (off & (RATE3 - 1))
        sel4 = (query & (RATE4 - 1)) == (off & (RATE4 - 1))
        key4 = (iota((far, tok), 0) & half) == 0
        near = (slot // quad) == (me // quad)
        count = jnp.where(near & sel3, 1.0, 0.0) + jnp.where(key4 & sel4, 1.0, 0.0)
        far_bias[h] = bias_of(jnp.where(slot < me, count, 0.0))

    each(1, kv_copies, "wait_recv")

    sums = [jnp.zeros((1, tok), jnp.float32) for _ in range(4)]
    stats = []
    far_keys = [per_head(kvbuf[0], h) for h in range(both)]
    far_values = [per_head(kvbuf[1], h) for h in range(both)]
    for h in range(both):
        peak, total, out = first_stats[h]
        score = dot_nt(far_keys[h], mats[2, h]) * scale2 + far_bias[h]
        top = jnp.maximum(peak, jnp.max(score, axis=0, keepdims=True))
        shrink = jnp.exp2(peak - top)
        held = jnp.exp2(score - top)
        total = total * shrink + jnp.sum(held, axis=0, keepdims=True)
        ratio = 1.0 / total
        far_weights[h] = held * ratio
        out = (out * shrink + dot_tn(far_values[h], held.astype(jnp.bfloat16))) * ratio
        grad = grads[h]
        sums[0] = sums[0] + jnp.sum(out, axis=0, keepdims=True)
        sums[1] = sums[1] + jnp.sum(out * out, axis=0, keepdims=True)
        sums[2] = sums[2] + jnp.sum(grad, axis=0, keepdims=True)
        sums[3] = sums[3] + jnp.sum(grad * out, axis=0, keepdims=True)
        stats.append((out, shrink * ratio, top + jnp.log2(total)))
    for at in range(4):
        hsend[at : at + 1, :] = sums[at]
    for copy in h_copies:
        copy.start()

    for h in range(both):
        weights[h] = weights[h] * stats[h][1]
    row = iota((2 * ROWS, both * tok), 0)
    column = iota((2 * ROWS, both * tok), 1)
    head_of = (row // half) & 1
    start = jnp.where(head_of == 0, wanted[0], wanted[1]) & (RATE4 - 1)
    place = (start ^ (RATE3 * (row // ROWS))) + RATE4 * (row & (half - 1)) + tok * head_of
    picker[...] = jnp.where(column == place, 1.0, 0.0).astype(jnp.bfloat16)
    for h in range(both):
        token = iota((tok, far), 0)
        column = iota((tok, far), 1)
        start = (wanted[h] & (RATE4 - 1)) ^ (2 * (column & half))
        hit = (token == start + RATE4 * (column & (half - 1))) & (column // ROWS == me)
        placer[:, pl.ds(h * far, far)] = jnp.where(hit, 1.0, 0.0).astype(jnp.bfloat16)

    each(0, q_copies, "wait_recv")
    late_queries = [per_head(qbuf[...], h) for h in range(both)]
    for h in range(both):
        off = wanted[h]
        slot = iota((tok, far), 1) // ROWS
        key = iota((tok, far), 0)
        sel3 = (key & (RATE3 - 1)) == (off & (RATE3 - 1))
        sel4 = (key & (RATE4 - 1)) == (off & (RATE4 - 1))
        query4 = (iota((tok, far), 1) & half) == 0
        near = (slot // quad) == (me // quad)
        count = jnp.where(near & sel3, 1.0, 0.0) + jnp.where(query4 & sel4, 1.0, 0.0)
        late_bias = bias_of(jnp.where(slot > me, count, 0.0))
        late_score[h] = dot_nt(mats[0, h], late_queries[h]) * scale2 + late_bias

    for copy in h_copies:
        copy.wait_recv()
    full = hsend[...]
    for at in range(heads):
        full = full + hbuf[at]
    full = full * (1.0 / features)
    centre = full[0:1]
    inverse = lax.rsqrt(full[1:2] - centre * centre + epsilon)
    first = full[2:3]
    second = inverse * (full[3:4] - centre * first)

    douts = []
    for h in range(both):
        out, _, lse = stats[h]
        normed = (out - centre) * inverse
        dout = (inverse * (grads[h] - first - normed * second)).astype(jnp.bfloat16)
        delta = jnp.sum(dout.astype(jnp.float32) * out, axis=0, keepdims=True)
        for at, rest in enumerate((lse, delta)):
            for piece in range(3):
                part = rest.astype(jnp.bfloat16).astype(jnp.float32)
                rest = rest - part
                line = 8 * h + 2 * piece + at
                rows_ref[line : line + 1, :] = part
        douts.append((dout, delta))
    chosen = dot_nt(picker[...], jnp.concatenate([item[0] for item in douts], axis=1))
    moved = dot_nn(rows_ref[...].astype(jnp.bfloat16), placer[...])
    moved = jnp.concatenate([moved[0:8, 0:far], moved[8:16, far : 2 * far]], axis=0)
    dosel[0:ROWS, :] = chosen[0:ROWS].astype(jnp.bfloat16)
    dosel[ROWS : 2 * ROWS, :] = moved.astype(jnp.bfloat16)
    dosel[2 * ROWS : 3 * ROWS, :] = chosen[ROWS : 2 * ROWS].astype(jnp.bfloat16)
    each(1, do_copies, "start")

    key_parts = []
    for h in range(both):
        dout, delta = douts[h]
        weight = weights[h]
        weight_grad = dot_nn(mats[1, h], dout)
        score_grad = (weight * (weight_grad - delta)).astype(jnp.bfloat16)
        value_part = dot_nt(weight.astype(jnp.bfloat16), dout)
        key_part = dot_nn(score_grad, mats[2, h])
        far_grad = dot_nn(far_values[h], dout)
        far_score = (far_weights[h] * (far_grad - delta)).astype(jnp.bfloat16)
        query_part = dot_tn(mats[0, h], score_grad) + dot_tn(far_keys[h], far_score)
        outwide[0, pl.ds(h, tok, stride=both), :] = (query_part * scale).T
        key_parts.append((key_part, value_part))
    dq_ref[...] = outwide[0].astype(jnp.bfloat16)

    each(0, do_copies, "wait_recv")

    arrived = dobuf[...].astype(jnp.float32)
    mixed = jnp.stack([arrived[:, 0:ROWS], arrived[:, 2 * ROWS : 3 * ROWS]], axis=1)
    lines = arrived[0, ROWS : 2 * ROWS]
    for at in range(1, seqs):
        lines = lines + arrived[at, ROWS : 2 * ROWS]
    for h in range(both):
        key_part, value_part = key_parts[h]
        late_douts = per_head(mixed, h)
        at = 8 * h
        lse = lines[at : at + 1] + lines[at + 2 : at + 3] + lines[at + 4 : at + 5]
        delta = lines[at + 1 : at + 2] + lines[at + 3 : at + 4] + lines[at + 5 : at + 6]
        weight = jnp.exp2(late_score[h] - lse)
        weight_grad = dot_nt(mats[1, h], late_douts)
        score_grad = (weight * (weight_grad - delta)).astype(jnp.bfloat16)
        value_part = value_part + dot_nn(weight.astype(jnp.bfloat16), late_douts)
        key_part = key_part + dot_nn(score_grad, late_queries[h])
        outwide[1, pl.ds(h, tok, stride=both), :] = key_part * scale
        outwide[2, pl.ds(h, tok, stride=both), :] = value_part
    dk_ref[...] = outwide[1].astype(jnp.bfloat16)
    dv_ref[...] = outwide[2].astype(jnp.bfloat16)

    each(0, kv_copies, "wait_send")
    each(1, q_copies, "wait_send")
    each(1, do_copies, "wait_send")
    for copy in h_copies:
        copy.wait_send()


def place_outputs(dq_ref, dk_ref, dv_ref, dq_hbm, dk_hbm, dv_hbm, sem):
    copies = [
        pltpu.make_async_copy(source, target, sem.at[at])
        for at, (source, target) in enumerate(
            ((dq_ref, dq_hbm), (dk_ref, dk_hbm), (dv_ref, dv_hbm))
        )
    ]
    for copy in copies:
        copy.start()
    for copy in copies:
        copy.wait()


def fused_shards(query_rows, key_rows, value_rows, cotangent, norm_gain, offsets):
    tok, both, size = query_rows.shape
    seqs = lax.axis_size("seq")
    heads = lax.axis_size("head")
    seg1 = tok * seqs // RATE4
    far = seqs * ROWS
    flat = (both * tok, size)
    low, full = jnp.bfloat16, jnp.float32
    vmem = pl.BlockSpec(memory_space=pltpu.VMEM)
    hbm = pl.BlockSpec(memory_space=pltpu.HBM)
    outs = pl.pallas_call(
        functools.partial(fused, seqs, heads, seg1, both * size * heads),
        out_shape=[jax.ShapeDtypeStruct(flat, low)] * 3,
        in_specs=[hbm] * 6,
        out_specs=[vmem] * 3,
        scratch_shapes=[
            pltpu.SMEM((both,), jnp.int32),
            pltpu.VMEM((both, size), full),
            pltpu.VMEM((4,) + flat, low),
            pltpu.VMEM((4,) + flat, full),
            pltpu.VMEM((3, both, tok, size), low),
            pltpu.VMEM((both, size, tok), full),
            pltpu.VMEM((both, tok, tok), full),
            pltpu.VMEM((both, far, tok), full),
            pltpu.VMEM((both, tok, tok), full),
            pltpu.VMEM((both, far, tok), full),
            pltpu.VMEM((both, tok, far), full),
            pltpu.VMEM((2 * ROWS, both * tok), low),
            pltpu.VMEM((tok, both * far), low),
            pltpu.VMEM((2, 2 * ROWS, size), low),
            pltpu.VMEM((2 * ROWS, size), low),
            pltpu.VMEM((3 * ROWS, size), low),
            pltpu.VMEM((2, seqs, 2 * ROWS, size), low),
            pltpu.VMEM((seqs, 2 * ROWS, size), low),
            pltpu.VMEM((seqs, 3 * ROWS, size), low),
            pltpu.VMEM((4, tok), full),
            pltpu.VMEM((heads, 4, tok), full),
            pltpu.VMEM((8 * both, tok), full),
            pltpu.VMEM((3,) + flat, full),
            pltpu.SemaphoreType.DMA((6,)),
        ]
        + [pltpu.SemaphoreType.DMA((seqs - 1,))] * 6
        + [pltpu.SemaphoreType.DMA((heads - 1,))] * 2,
        compiler_params=pltpu.CompilerParams(
            collective_id=0, has_side_effects=True, vmem_limit_bytes=VMEM_BYTES
        ),
        name="fused_backward",
    )(
        offsets,
        query_rows.reshape(flat),
        key_rows.reshape(flat),
        value_rows.reshape(flat),
        cotangent.reshape(flat),
        norm_gain,
    )
    outs = pl.pallas_call(
        place_outputs,
        out_shape=[jax.ShapeDtypeStruct(flat, low)] * 3,
        in_specs=[vmem] * 3,
        out_specs=[hbm] * 3,
        scratch_shapes=[pltpu.SemaphoreType.DMA((3,))],
        name="place_outputs",
    )(*outs)
    return tuple(out.reshape(query_rows.shape) for out in outs)


def fits(mesh, tok, both, size):
    seqs = mesh.shape["seq"]
    seg1 = tok * seqs // RATE4
    return (
        tok == ROWS * RATE3
        and size == 128
        and both == 2
        and seqs * ROWS == 128
        and (RATE3 * seg1 // tok) & (RATE3 * seg1 // tok - 1) == 0
        and tok % (RATE2 * seg1) == 0
        and (RATE3 * seg1) % tok == 0
        and tok // seg1 <= 64
    )


def solution(mesh):
    placed = (
        P("seq", "head", None),
        P("seq", "head", None),
        P("seq", "head", None),
        P("seq", "head", None),
        P("head", None),
        P("head"),
    )

    def run(query_rows, key_rows, value_rows, cotangent, norm_gain, offsets):
        tokens, heads, size = query_rows.shape
        small = fits(mesh, tokens // mesh.shape["seq"], heads // mesh.shape["head"], size)
        return jax.shard_map(
            fused_shards if small else shards,
            mesh=mesh,
            in_specs=placed,
            out_specs=(P("seq", "head", None), P("seq", "head", None), P("seq", "head", None)),
            check_vma=False,
        )(query_rows, key_rows, value_rows, cotangent, norm_gain, offsets)

    return run
```

profile of v0, /device:TPU:0, one launch (start us, length us, event | category | flops | bytes accessed | tf_op | source)
XLA Modules:
  0.0 22.1 jit_solution(10130466387539690736)
XLA Ops:
  0.6 0.0 copy-start.3
  0.6 0.0 copy-start.4
  0.7 0.7 %copy-done.3 = f32[2,128]{1,0:T(2,128)S(1)} copy-done((f32[2,128]{1,0:T(2,128)S(1)}, f32[2,128]{1,0:T(2,128)}, u32[]{:S(2)}) %copy-start.3) | copy-done | bytes 1048
  1.3 0.0 copy-done.4
  1.3 17.0 %fused_backward.1 = (bf16[512,128]{1,0:T(8,128)(2,1)S(1)}, bf16[512,128]{1,0:T(8,128)(2,1)S(1)}, bf16[512,128]{1,0:T(8,128)(2,1)S(1)}) custom-call(s32[2]{0:T(128)S(1)} %copy-done.4, bf16[512,128]{1,0:T(8,128)(2,1)} %bitcast.7, bf16[512,128]{1,0:T(8,128)(2,1)} %bitcast.8, bf16[512,128]{1,0:T(8,128)(2,1)} %bitcast.9, bf16[512,128]{1,0:T(8,128)(2,1)} %bitcast.10, ...), custom_call_target="tpu_custom_call" | custom-call | tf_op jit(solution)/shard_map/fused_backward/pallas_call | solution.py:696
  18.3 0.0 copy-start
  18.3 0.6 %copy-done = bf16[512,128]{1,0:T(8,128)(2,1)} copy-done((bf16[512,128]{1,0:T(8,128)(2,1)}, bf16[512,128]{1,0:T(8,128)(2,1)S(1)}, u32[]{:S(2)}) %copy-start) | copy-done | bytes 131096
  19.0 0.0 copy-start.1
  19.0 0.6 %copy-done.1 = bf16[512,128]{1,0:T(8,128)(2,1)} copy-done((bf16[512,128]{1,0:T(8,128)(2,1)}, bf16[512,128]{1,0:T(8,128)(2,1)S(1)}, u32[]{:S(2)}) %copy-start.1) | copy-done | bytes 131096
  19.6 0.0 copy-start.2
  19.6 0.6 %copy-done.2 = bf16[512,128]{1,0:T(8,128)(2,1)} copy-done((bf16[512,128]{1,0:T(8,128)(2,1)}, bf16[512,128]{1,0:T(8,128)(2,1)S(1)}, u32[]{:S(2)}) %copy-start.2) | copy-done | bytes 131096
  20.3 1.8 %place_outputs.1 = (bf16[512,128]{1,0:T(8,128)(2,1)}, bf16[512,128]{1,0:T(8,128)(2,1)}, bf16[512,128]{1,0:T(8,128)(2,1)}) custom-call(bf16[512,128]{1,0:T(8,128)(2,1)} %copy-done, bf16[512,128]{1,0:T(8,128)(2,1)} %copy-done.1, bf16[512,128]{1,0:T(8,128)(2,1)} %copy-done.2), custom_call_target="tpu_custom_call" | custom-call | tf_op jit(solution)/shard_map/place_outputs/pallas_call | solution.py:741
Async XLA Ops:
  0.6 0.7 %copy-start.3 = (f32[2,128]{1,0:T(2,128)S(1)}, f32[2,128]{1,0:T(2,128)}, u32[]{:S(2)}) copy-start(f32[2,128]{1,0:T(2,128)} %gain_hbm.1) | copy-start | bytes 3076
  0.6 0.7 %copy-start.4 = (s32[2]{0:T(128)S(1)}, s32[2]{0:T(128)}, u32[]{:S(2)}) copy-start(s32[2]{0:T(128)} %off_hbm.1) | copy-start | bytes 28
  18.3 0.6 %copy-start = (bf16[512,128]{1,0:T(8,128)(2,1)}, bf16[512,128]{1,0:T(8,128)(2,1)S(1)}, u32[]{:S(2)}) copy-start(bf16[512,128]{1,0:T(8,128)(2,1)S(1)} %get-tuple-element.9.dq_ref) | copy-start | bytes 393220
  19.0 0.6 %copy-start.1 = (bf16[512,128]{1,0:T(8,128)(2,1)}, bf16[512,128]{1,0:T(8,128)(2,1)S(1)}, u32[]{:S(2)}) copy-start(bf16[512,128]{1,0:T(8,128)(2,1)S(1)} %get-tuple-element.10.dk_ref) | copy-start | bytes 393220
  19.6 0.6 %copy-start.2 = (bf16[512,128]{1,0:T(8,128)(2,1)}, bf16[512,128]{1,0:T(8,128)(2,1)S(1)}, u32[]{:S(2)}) copy-start(bf16[512,128]{1,0:T(8,128)(2,1)S(1)} %get-tuple-element.11.dv_ref) | copy-start | bytes 393220
where the time goes:
time: 22.2 us; the launch traced here: 22.1 us
  Pallas kernels  18.8 us (85%)
  local copies, waits for them, and re-layouts  2.6 us (12%)
  between operations  0.67 us (3%)
    pallas_call x1, Pallas kernels, fused_shards(): pl.pallas_call(functools.partial(fused, seqs, heads, seg1, both * size *...  17 us
    unnamed x10, local copies, waits for them, and re-layouts  2.6 us
    pallas_call x1, Pallas kernels, fused_shards(): pl.pallas_call(place_outputs, out_shape=[jax.ShapeDtypeStruct(flat, low)]...  1.79 us

commit v1 on v0

--- a/solution.py
+++ b/solution.py
@@ -491,41 +491,6 @@
         count = dot_nt(marked, marked)
         bias[h] = bias_of(jnp.where(causal, count, 0.0))
 
-    for at in range(2):
-        loads[1 + at].wait()
-        wide[at] = xin[at].astype(jnp.float32)
-        for g in range(2):
-            kvsel[at, pl.ds(g * ROWS, ROWS), :] = select(at, g)
-    pl.semaphore_wait(barrier, seqs + heads - 2)
-    each(0, kv_copies, "start")
-
-    loads[3].wait()
-    wide[2] = xin[2].astype(jnp.float32)
-    for g in range(2):
-        qsel[pl.ds(g * ROWS, ROWS), :] = select(2, g)
-    each(1, q_copies, "start")
-
-    for at in range(3):
-        for h in range(both):
-            mats[at, h] = wide[at, pl.ds(h, tok, stride=both), :].astype(jnp.bfloat16)
-
-    first_stats = []
-    for h in range(both):
-        score = dot_nt(mats[0, h], mats[2, h]) * scale2 + bias[h]
-        peak = jnp.max(score, axis=0, keepdims=True)
-        held = jnp.exp2(score - peak)
-        weights[h] = held
-        total = jnp.sum(held, axis=0, keepdims=True)
-        out = dot_tn(mats[1, h], held.astype(jnp.bfloat16))
-        first_stats.append((peak, total, out))
-
-    loads[4].wait()
-    loads[5].wait()
-    wide[3] = xin[3].astype(jnp.float32)
-    for h in range(both):
-        grad = wide[3, pl.ds(h, tok, stride=both), :] * gain_ref[h : h + 1, :]
-        grads[h] = grad.T
-
     for h in range(both):
         off = wanted[h]
         slot = iota((far, tok), 0) // ROWS
@@ -536,6 +501,41 @@
         near = (slot // quad) == (me // quad)
         count = jnp.where(near & sel3, 1.0, 0.0) + jnp.where(key4 & sel4, 1.0, 0.0)
         far_bias[h] = bias_of(jnp.where(slot < me, count, 0.0))
+
+    for at in range(2):
+        loads[1 + at].wait()
+        wide[at] = xin[at].astype(jnp.float32)
+        for g in range(2):
+            kvsel[at, pl.ds(g * ROWS, ROWS), :] = select(at, g)
+    pl.semaphore_wait(barrier, seqs + heads - 2)
+    each(0, kv_copies, "start")
+
+    loads[3].wait()
+    wide[2] = xin[2].astype(jnp.float32)
+    for g in range(2):
+        qsel[pl.ds(g * ROWS, ROWS), :] = select(2, g)
+    each(1, q_copies, "start")
+
+    for at in range(3):
+        for h in range(both):
+            mats[at, h] = wide[at, pl.ds(h, tok, stride=both), :].astype(jnp.bfloat16)
+
+    first_stats = []
+    for h in range(both):
+        score = dot_nt(mats[0, h], mats[2, h]) * scale2 + bias[h]
+        peak = jnp.max(score, axis=0, keepdims=True)
+        held = jnp.exp2(score - peak)
+        weights[h] = held
+        total = jnp.sum(held, axis=0, keepdims=True)
+        out = dot_tn(mats[1, h], held.astype(jnp.bfloat16))
+        first_stats.append((peak, total, out))
+
+    loads[4].wait()
+    loads[5].wait()
+    wide[3] = xin[3].astype(jnp.float32)
+    for h in range(both):
+        grad = wide[3, pl.ds(h, tok, stride=both), :] * gain_ref[h : h + 1, :]
+        grads[h] = grad.T
 
     each(1, kv_copies, "wait_recv")
 
@@ -744,6 +744,7 @@
         in_specs=[vmem] * 3,
         out_specs=[hbm] * 3,
         scratch_shapes=[pltpu.SemaphoreType.DMA((3,))],
+        compiler_params=pltpu.CompilerParams(vmem_limit_bytes=1024 * 1024),
         name="place_outputs",
     )(*outs)
     return tuple(out.reshape(query_rows.shape) for out in outs)

time: 22.2 us -> 19.3 us (0.87)
  local copies, waits for them, and re-layouts: 2.6 us -> 0.67 us
  Pallas kernels: 18.8 us -> 17.8 us
    unnamed x10 -> x4, local copies, waits for them, and re-layouts: 2.6 us -> 0.67 us
    pallas_call x1, Pallas kernels: 1.79 us -> 0.77 us  [fused_shards(): pl.pallas_call(place_outputs, out_shape=[jax.ShapeDtypeStruct(flat, low)]...]
where the time goes in v1:
time: 19.3 us; the launch traced here: 19.1 us
  Pallas kernels  17.8 us (92%)
  local copies, waits for them, and re-layouts  0.67 us (3%)
  between operations  0.66 us (3%)
    pallas_call x1, Pallas kernels, fused_shards(): pl.pallas_call(functools.partial(fused, seqs, heads, seg1, both * size *...  17 us
    pallas_call x1, Pallas kernels, fused_shards(): pl.pallas_call(place_outputs, out_shape=[jax.ShapeDtypeStruct(flat, low)]...  0.77 us
    unnamed x4, local copies, waits for them, and re-layouts  0.67 us

profile of v1, /device:TPU:0, one launch (start us, length us, event | category | flops | bytes accessed | tf_op | source)
XLA Modules:
  0.0 19.1 jit_solution(3689657344697004714)
XLA Ops:
  0.6 0.0 copy-start
  0.6 0.0 copy-start.1
  0.7 0.7 %copy-done = f32[2,128]{1,0:T(2,128)S(1)} copy-done((f32[2,128]{1,0:T(2,128)S(1)}, f32[2,128]{1,0:T(2,128)}, u32[]{:S(2)}) %copy-start) | copy-done | bytes 1048
  1.3 0.0 copy-done.1
  1.3 17.0 %fused_backward.1 = (bf16[512,128]{1,0:T(8,128)(2,1)S(1)}, bf16[512,128]{1,0:T(8,128)(2,1)S(1)}, bf16[512,128]{1,0:T(8,128)(2,1)S(1)}) custom-call(s32[2]{0:T(128)S(1)} %copy-done.1, bf16[512,128]{1,0:T(8,128)(2,1)} %bitcast.7, bf16[512,128]{1,0:T(8,128)(2,1)} %bitcast.8, bf16[512,128]{1,0:T(8,128)(2,1)} %bitcast.9, bf16[512,128]{1,0:T(8,128)(2,1)} %bitcast.10, ...), custom_call_target="tpu_custom_call" | custom-call | tf_op jit(solution)/shard_map/fused_backward/pallas_call | solution.py:696
  18.3 0.8 %place_outputs.1 = (bf16[512,128]{1,0:T(8,128)(2,1)}, bf16[512,128]{1,0:T(8,128)(2,1)}, bf16[512,128]{1,0:T(8,128)(2,1)}) custom-call(bf16[512,128]{1,0:T(8,128)(2,1)S(1)} %get-tuple-element.9.dq_ref, bf16[512,128]{1,0:T(8,128)(2,1)S(1)} %get-tuple-element.10.dk_ref, bf16[512,128]{1,0:T(8,128)(2,1)S(1)} %get-tuple-element.11.dv_ref), custom_call_target="tpu_custom_call" | custom-call | tf_op jit(solution)/shard_map/place_outputs/pallas_call | solution.py:741
Async XLA Ops:
  0.6 0.7 %copy-start = (f32[2,128]{1,0:T(2,128)S(1)}, f32[2,128]{1,0:T(2,128)}, u32[]{:S(2)}) copy-start(f32[2,128]{1,0:T(2,128)} %gain_hbm.1) | copy-start | bytes 3076
  0.6 0.7 %copy-start.1 = (s32[2]{0:T(128)S(1)}, s32[2]{0:T(128)}, u32[]{:S(2)}) copy-start(s32[2]{0:T(128)} %off_hbm.1) | copy-start | bytes 28

commit v2 on v1

--- a/solution.py
+++ b/solution.py
@@ -514,7 +514,6 @@
     wide[2] = xin[2].astype(jnp.float32)
     for g in range(2):
         qsel[pl.ds(g * ROWS, ROWS), :] = select(2, g)
-    each(1, q_copies, "start")
 
     for at in range(3):
         for h in range(both):
@@ -563,6 +562,7 @@
         hsend[at : at + 1, :] = sums[at]
     for copy in h_copies:
         copy.start()
+    each(1, q_copies, "start")
 
     for h in range(both):
         weights[h] = weights[h] * stats[h][1]
@@ -579,19 +579,15 @@
         hit = (token == start + RATE4 * (column & (half - 1))) & (column // ROWS == me)
         placer[:, pl.ds(h * far, far)] = jnp.where(hit, 1.0, 0.0).astype(jnp.bfloat16)
 
-    each(0, q_copies, "wait_recv")
-    late_queries = [per_head(qbuf[...], h) for h in range(both)]
-    for h in range(both):
-        off = wanted[h]
-        slot = iota((tok, far), 1) // ROWS
-        key = iota((tok, far), 0)
-        sel3 = (key & (RATE3 - 1)) == (off & (RATE3 - 1))
-        sel4 = (key & (RATE4 - 1)) == (off & (RATE4 - 1))
-        query4 = (iota((tok, far), 1) & half) == 0
-        near = (slot // quad) == (me // quad)
-        count = jnp.where(near & sel3, 1.0, 0.0) + jnp.where(query4 & sel4, 1.0, 0.0)
-        late_bias = bias_of(jnp.where(slot > me, count, 0.0))
-        late_score[h] = dot_nt(mats[0, h], late_queries[h]) * scale2 + late_bias
+    def put_pieces(h, at, rest):
+        for piece in range(3):
+            part = rest.astype(jnp.bfloat16).astype(jnp.float32)
+            rest = rest - part
+            line = 8 * h + 2 * piece + at
+            rows_ref[line : line + 1, :] = part
+
+    for h in range(both):
+        put_pieces(h, 0, stats[h][2])
 
     for copy in h_copies:
         copy.wait_recv()
@@ -606,16 +602,11 @@
 
     douts = []
     for h in range(both):
-        out, _, lse = stats[h]
+        out = stats[h][0]
         normed = (out - centre) * inverse
         dout = (inverse * (grads[h] - first - normed * second)).astype(jnp.bfloat16)
         delta = jnp.sum(dout.astype(jnp.float32) * out, axis=0, keepdims=True)
-        for at, rest in enumerate((lse, delta)):
-            for piece in range(3):
-                part = rest.astype(jnp.bfloat16).astype(jnp.float32)
-                rest = rest - part
-                line = 8 * h + 2 * piece + at
-                rows_ref[line : line + 1, :] = part
+        put_pieces(h, 1, delta)
         douts.append((dout, delta))
     chosen = dot_nt(picker[...], jnp.concatenate([item[0] for item in douts], axis=1))
     moved = dot_nn(rows_ref[...].astype(jnp.bfloat16), placer[...])
@@ -639,6 +630,20 @@
         outwide[0, pl.ds(h, tok, stride=both), :] = (query_part * scale).T
         key_parts.append((key_part, value_part))
     dq_ref[...] = outwide[0].astype(jnp.bfloat16)
+
+    each(0, q_copies, "wait_recv")
+    late_queries = [per_head(qbuf[...], h) for h in range(both)]
+    for h in range(both):
+        off = wanted[h]
+        slot = iota((tok, far), 1) // ROWS
+        key = iota((tok, far), 0)
+        sel3 = (key & (RATE3 - 1)) == (off & (RATE3 - 1))
+        sel4 = (key & (RATE4 - 1)) == (off & (RATE4 - 1))
+        query4 = (iota((tok, far), 1) & half) == 0
+        near = (slot // quad) == (me // quad)
+        count = jnp.where(near & sel3, 1.0, 0.0) + jnp.where(query4 & sel4, 1.0, 0.0)
+        late_bias = bias_of(jnp.where(slot > me, count, 0.0))
+        late_score[h] = dot_nt(mats[0, h], late_queries[h]) * scale2 + late_bias
 
     each(0, do_copies, "wait_recv")
 

time: 19.3 us -> 19.3 us (level)
  no operation moved by 1% of the time
where the time goes in v2:
time: 19.3 us; the launch traced here: 19.1 us
  Pallas kernels  17.8 us (92%)
  local copies, waits for them, and re-layouts  0.67 us (3%)
  between operations  0.66 us (3%)
    pallas_call x1, Pallas kernels, fused_shards(): pl.pallas_call(functools.partial(fused, seqs, heads, seg1, both * size *...  17 us
    pallas_call x1, Pallas kernels, fused_shards(): pl.pallas_call(place_outputs, out_shape=[jax.ShapeDtypeStruct(flat, low)]...  0.77 us
    unnamed x4, local copies, waits for them, and re-layouts  0.67 us

profile of v2, /device:TPU:0, one launch (start us, length us, event | category | flops | bytes accessed | tf_op | source)
XLA Modules:
  0.0 19.1 jit_solution(3984546441516688141)
XLA Ops:
  0.6 0.0 copy-start
  0.6 0.0 copy-start.1
  0.7 0.7 %copy-done = f32[2,128]{1,0:T(2,128)S(1)} copy-done((f32[2,128]{1,0:T(2,128)S(1)}, f32[2,128]{1,0:T(2,128)}, u32[]{:S(2)}) %copy-start) | copy-done | bytes 1048
  1.3 0.0 copy-done.1
  1.3 17.0 %fused_backward.1 = (bf16[512,128]{1,0:T(8,128)(2,1)S(1)}, bf16[512,128]{1,0:T(8,128)(2,1)S(1)}, bf16[512,128]{1,0:T(8,128)(2,1)S(1)}) custom-call(s32[2]{0:T(128)S(1)} %copy-done.1, bf16[512,128]{1,0:T(8,128)(2,1)} %bitcast.7, bf16[512,128]{1,0:T(8,128)(2,1)} %bitcast.8, bf16[512,128]{1,0:T(8,128)(2,1)} %bitcast.9, bf16[512,128]{1,0:T(8,128)(2,1)} %bitcast.10, ...), custom_call_target="tpu_custom_call" | custom-call | tf_op jit(solution)/shard_map/fused_backward/pallas_call | solution.py:701
  18.4 0.8 %place_outputs.1 = (bf16[512,128]{1,0:T(8,128)(2,1)}, bf16[512,128]{1,0:T(8,128)(2,1)}, bf16[512,128]{1,0:T(8,128)(2,1)}) custom-call(bf16[512,128]{1,0:T(8,128)(2,1)S(1)} %get-tuple-element.9.dq_ref, bf16[512,128]{1,0:T(8,128)(2,1)S(1)} %get-tuple-element.10.dk_ref, bf16[512,128]{1,0:T(8,128)(2,1)S(1)} %get-tuple-element.11.dv_ref), custom_call_target="tpu_custom_call" | custom-call | tf_op jit(solution)/shard_map/place_outputs/pallas_call | solution.py:746
Async XLA Ops:
  0.6 0.7 %copy-start = (f32[2,128]{1,0:T(2,128)S(1)}, f32[2,128]{1,0:T(2,128)}, u32[]{:S(2)}) copy-start(f32[2,128]{1,0:T(2,128)} %gain_hbm.1) | copy-start | bytes 3076
  0.6 0.7 %copy-start.1 = (s32[2]{0:T(128)S(1)}, s32[2]{0:T(128)}, u32[]{:S(2)}) copy-start(s32[2]{0:T(128)} %off_hbm.1) | copy-start | bytes 28
